TPU v7x, 32 devices: a whole 2x2x4 slice. The times are simulated.
32 devices in a mesh: clip: 16 (over z, x, core), tile: 2 (over y).
Axes of the slice: x: 2, y: 2, z: 4, core: 2. Of those that a mesh axis runs over, the one named last changes fastest.
Arguments:
- latents: bfloat16 [32, 40, 64, 320], P('clip', 'tile'), may hold values from -64 to 64
- lengths: int32 [16], P('clip'), may hold values from 1 to 2, as said below
- context: int32 [8], replicated, may hold values from 0 to 31, as said below
- gain_first: float32 [320], replicated, may hold values from 0.25 to 1.75
- conv_first: bfloat16 [3, 3, 320, 320], replicated, may hold values from -0.109375 to 0.109375
- gain_second: float32 [320], replicated, may hold values from 0.25 to 1.75
- conv_second: bfloat16 [3, 3, 320, 320], replicated, may hold values from -0.109375 to 0.109375
- time_weight: bfloat16 [3, 320, 320], replicated, may hold values from -0.1875 to 0.1875
- attn_gain: float32 [320], replicated, may hold values from 0.25 to 1.75
- w_qkv: bfloat16 [320, 960], replicated, may hold values from -2 to 2
- w_out: bfloat16 [320, 320], replicated, may hold values from -0.3125 to 0.3125
Outputs:
- block_out: bfloat16 [32, 40, 64, 320], P('clip', 'tile')
Inputs may be any that keep to these rules, and one draw needn't show every extreme that they name: `lengths`: the last clip is full with 2 live frames and some other clip has 1. The context frames lie in distinct clips; each names slot c * 2 + f of a live frame f < lengths[c].
All inputs are finite; a program needn't handle non-finite values.
Results may differ from a plain program's by a relative error of at most 0.011.
Values may be sent and summed in bfloat16 or wider, within the bound.
No kernel may reach another device: no remote copies, remote signals or barrier semaphores. Data moves between devices by JAX's collectives and lax.ppermute only.
A program may use at most 128 MiB of HBM per device.

v0:
```python
import jax
import jax.numpy as jnp
from jax import lax
from jax.sharding import PartitionSpec as P

HEAD_DIM = 64
GROUPS = 32
H = 40
W = 64


EPS = 1e-05
MASKED = -1e30


def with_halo(block, sides, width):
    for axis, dim in sides:
        count = lax.axis_size(axis)
        forward = [(i, i + 1) for i in range(count - 1)]
        backward = [(target, source) for source, target in forward]
        low = lax.ppermute(
            lax.slice_in_dim(block, block.shape[dim] - width, None, axis=dim), axis, forward
        )
        high = lax.ppermute(lax.slice_in_dim(block, 0, width, axis=dim), axis, backward)
        block = jnp.concatenate([low, block, high], axis=dim)
    return block


def from_behind(block, axis, distance):
    devices = range(lax.axis_size(axis))
    route = [(i - distance, i) for i in devices if i - distance in devices]
    return lax.ppermute(block, axis, route)


def finish(total_sum, square_sum, gain):
    group_width = gain.shape[0] // GROUPS
    count = H * W * group_width
    centre = total_sum / count
    spread = square_sum / count - centre * centre
    inverse = lax.rsqrt(spread + EPS)
    scale = jnp.repeat(inverse, group_width, axis=1) * gain[None, :]
    shift = -jnp.repeat(centre, group_width, axis=1) * scale
    return (scale, shift)


def activate(source, scale, shift):
    return jax.nn.silu(
        source.astype(jnp.float32) * scale[:, None, None, :] + shift[:, None, None, :]
    ).astype(jnp.bfloat16)


def convolve(padded, weights):
    wide = jnp.pad(padded, ((0, 0), (0, 0), (1, 1), (0, 0)))
    row_count = padded.shape[1] - 2
    col_count = padded.shape[2]
    result = jnp.zeros((padded.shape[0], row_count, col_count, weights.shape[-1]), jnp.float32)
    for row_step in range(3):
        for col_step in range(3):
            window = wide[:, row_step : row_step + row_count, col_step : col_step + col_count, :]
            result = result + jnp.dot(
                window, weights[row_step, col_step], preferred_element_type=jnp.float32
            )
    return result


def conv_section(source, gain, weights):
    frame_count, tile_rows, col_count, channels = source.shape
    group_width = channels // GROUPS
    values = source.astype(jnp.float32).reshape(
        frame_count, tile_rows * col_count, GROUPS, group_width
    )
    total_sum, square_sum = lax.psum(
        (jnp.sum(values, axis=(1, 3)), jnp.sum(values * values, axis=(1, 3))), "tile"
    )
    scale, shift = finish(total_sum, square_sum, gain)
    activated = activate(source, scale, shift)
    padded = with_halo(activated, (("tile", 1),), 1)
    return convolve(padded, weights)


def layer_norm(source, gain):
    values = source.astype(jnp.float32)
    centre = jnp.mean(values, axis=-1, keepdims=True)
    spread = jnp.mean((values - centre) ** 2, axis=-1, keepdims=True)
    return ((values - centre) * lax.rsqrt(spread + EPS) * gain).astype(jnp.bfloat16)


def attend(packed, shared_kv, live_count):
    frame_count, cell_count, packed_width = packed.shape
    channels = packed_width // 3
    head_count = channels // HEAD_DIM
    shape_local = (frame_count, cell_count, head_count, HEAD_DIM)
    shape_shared = (shared_kv.shape[0], cell_count, head_count, HEAD_DIM)
    queries = packed[..., :channels].reshape(shape_local)
    keys_local = packed[..., channels : 2 * channels].reshape(shape_local)
    values_local = packed[..., 2 * channels :].reshape(shape_local)
    keys_shared = shared_kv[..., :channels].reshape(shape_shared)
    values_shared = shared_kv[..., channels:].reshape(shape_shared)
    score_scale = HEAD_DIM ** (-0.5)
    near_scores = (
        jnp.einsum("fnhd,gnhd->nhfg", queries, keys_local, preferred_element_type=jnp.float32)
        * score_scale
    )
    visible = jnp.arange(frame_count) < live_count
    near_scores = jnp.where(visible, near_scores, MASKED)
    far_scores = (
        jnp.einsum("fnhd,jnhd->nhfj", queries, keys_shared, preferred_element_type=jnp.float32)
        * score_scale
    )
    ceiling = jnp.maximum(jnp.max(near_scores, axis=-1), jnp.max(far_scores, axis=-1))[..., None]
    near_exp = jnp.exp(near_scores - ceiling)
    far_exp = jnp.exp(far_scores - ceiling)
    normaliser = jnp.sum(near_exp, axis=-1, keepdims=True) + jnp.sum(
        far_exp, axis=-1, keepdims=True
    )
    near_weight = (near_exp / normaliser).astype(jnp.bfloat16)
    far_weight = (far_exp / normaliser).astype(jnp.bfloat16)
    result = jnp.einsum(
        "nhfg,gnhd->fnhd", near_weight, values_local, preferred_element_type=jnp.float32
    )
    result = result + jnp.einsum(
        "nhfj,jnhd->fnhd", far_weight, values_shared, preferred_element_type=jnp.float32
    )
    return result.reshape(frame_count, cell_count, channels).astype(jnp.bfloat16)


def local(
    latents,
    lengths,
    context,
    gain_first,
    conv_first,
    gain_second,
    conv_second,
    time_weight,
    attn_gain,
    w_qkv,
    w_out,
):
    frame_count, tile_rows, col_count, channels = latents.shape
    hidden_one = conv_section(latents, gain_first, conv_first).astype(jnp.bfloat16)
    res_one = (
        latents.astype(jnp.float32) + conv_section(hidden_one, gain_second, conv_second)
    ).astype(jnp.bfloat16)
    moving = jax.nn.silu(res_one.astype(jnp.float32)).astype(jnp.bfloat16)
    live_count = lengths[0]
    final_frame = lax.dynamic_index_in_dim(moving, live_count - 1, 0, keepdims=False)
    prior = from_behind(final_frame, "clip", 1)
    later = from_behind(moving[0], "clip", -1)
    backward = jnp.concatenate([prior[None], moving[:-1]], axis=0)
    forward = jnp.concatenate([moving[1:], jnp.zeros_like(moving[:1])], axis=0)
    slots = jnp.arange(frame_count)
    forward = jnp.where((slots == live_count - 1)[:, None, None, None], later[None], forward)
    mixed = res_one.astype(jnp.float32) + jnp.dot(
        backward, time_weight[0], preferred_element_type=jnp.float32
    )
    mixed = mixed + jnp.dot(moving, time_weight[1], preferred_element_type=jnp.float32)
    mixed = mixed + jnp.dot(forward, time_weight[2], preferred_element_type=jnp.float32)
    res_two = mixed.astype(jnp.bfloat16)
    cell_count = tile_rows * col_count
    normed = layer_norm(res_two, attn_gain).reshape(frame_count, cell_count, channels)
    packed = jnp.dot(normed, w_qkv, preferred_element_type=jnp.float32).astype(jnp.bfloat16)
    selector = (context[:, None] == lax.axis_index("clip") * frame_count + slots[None, :]).astype(
        jnp.bfloat16
    )
    picked = jnp.einsum("jf,fnc->jnc", selector, normed, preferred_element_type=jnp.float32)
    picked = lax.psum(picked.astype(jnp.bfloat16), "clip")
    shared_kv = jnp.dot(picked, w_qkv[:, channels:], preferred_element_type=jnp.float32).astype(
        jnp.bfloat16
    )
    attended = attend(packed, shared_kv, live_count)
    result = res_two.astype(jnp.float32).reshape(frame_count, cell_count, channels)
    result = result + jnp.dot(attended, w_out, preferred_element_type=jnp.float32)
    result = jnp.where((slots < live_count)[:, None, None], result, 0.0)
    return result.astype(jnp.bfloat16).reshape(frame_count, tile_rows, col_count, channels)


def solution(mesh):
    placed = (P("clip", "tile", None, None), P("clip"), P(), P(), P(), P(), P(), P(), P(), P(), P())
    return jax.shard_map(
        local, mesh=mesh, in_specs=placed, out_specs=P("clip", "tile", None, None), check_vma=False
    )
```

profile of v0, /device:TPU:0, one launch (start us, length us, event | category | flops | bytes accessed | tf_op | source)
XLA Modules:
  0.0 462.2 jit_solution(16400040529617497910)
XLA Ops:
  9.1 5.9 %all-reduce.4 = (f32[2,32]{1,0:T(2,128)S(1)}, f32[2,32]{1,0:T(2,128)S(1)}) all-reduce(f32[2,32]{1,0:T(2,128)S(1)} %reduce_sum.105, f32[2,32]{1,0:T(2,128)S(1)} %reduce_sum.83), channel_id=1, replica_groups=mesh['clip'=16,'tile'=2] {'tile'}, use_global_device_ids=true, to_apply=%region_5.6 | all-reduce | flops 128 | bytes 1024 | tf_op jit(solution)/shard_map/psum | solution.py:72
  20.1 4.6 collective-permute-start
  52.2 9.5 %fusion.3 = (f32[2,320]{1,0:T(2,128)S(1)}, f32[2,320]{1,0:T(2,128)S(1)}, bf16[2,20,64,320]{3,2,1,0:T(8,128)(2,1)S(1)}) fusion(bf16[3,3,320,320]{3,2,1,0:T(8,128)(2,1)} %param.15, bf16[2,22,66,320]{3,2,1,0:T(8,128)(2,1)S(1)} %fusion.36, f32[2,20,64,320]{3,2,1,0:T(8,128)} %fusion.41, f32[2,20,64,320]{3,2,1,0:T(8,128)S(1)} %fusion.67, ...), kind=kOutput, calls=%fused_computation.22 | convolution fusion | flops 534936320 | bytes 35312640 | tf_op jit(solution)/shard_map/dot_general | solution.py:60
  62.0 4.9 %all-reduce.3 = (f32[2,32]{1,0:T(2,128)S(1)}, f32[2,32]{1,0:T(2,128)S(1)}) all-reduce(f32[2,32]{1,0:T(2,128)S(1)} %reduce_sum.111, f32[2,32]{1,0:T(2,128)S(1)} %reduce_sum.108), channel_id=1, replica_groups=mesh['clip'=16,'tile'=2] {'tile'}, use_global_device_ids=true, to_apply=%region_11.12 | all-reduce | flops 128 | bytes 1024 | tf_op jit(solution)/shard_map/psum | solution.py:72
  69.9 4.6 collective-permute-start.2
  102.5 12.9 %fusion.14 = (bf16[2,20,64,320]{3,2,1,0:T(8,128)(2,1)S(1)}, bf16[2,20,64,320]{3,2,1,0:T(8,128)(2,1)}) fusion(bf16[3,3,320,320]{3,2,1,0:T(8,128)(2,1)S(1)} %copy-done.10, bf16[2,22,66,320]{3,2,1,0:T(8,128)(2,1)S(1)} %select_maximum_fusion, f32[2,20,64,320]{3,2,1,0:T(8,128)} %fusion.49, f32[2,20,64,320]{3,2,1,0:T(8,128)} %fusion.55, ...), kind=kOutput, calls=%fused_computation.33 | convolution fusion | flops 538214400 | bytes 33669120 | tf_op jit(solution)/shard_map/dot_general | solution.py:60
  131.4 6.7 %copy.73 = bf16[2,1280,320]{1,0,2:T(2,128)(2,1)} copy(bf16[2,1280,320]{2,1,0:T(8,128)(2,1)} %bitcast.202) | data formatting | bytes 3276800 | tf_op jit(solution)/shard_map/reshape | solution.py:161
  138.1 5.8 %convolution_convert_fusion.1 = bf16[8,1280,320]{1,0,2:T(8,128)(2,1)} fusion(bf16[2,1280,320]{1,0,2:T(2,128)(2,1)} %copy.73, s32[8]{0:T(128)S(1)} %copy-done.17, s32[2]{0:T(128)S(1)} %iota_add_fusion), kind=kOutput, calls=%fused_computation.11 | convolution fusion | flops 16384016 | bytes 8192040 | tf_op jit(solution)/shard_map/jf,fnc->jnc/dot_general | solution.py:166
  152.3 7.5 %copy.80 = bf16[2,1280,5,64]{3,0,2,1:T(2,128)(2,1)} copy(bf16[2,1280,5,64]{1,3,2,0:T(8,128)(2,1)} %bitcast.211) | data formatting | bytes 3276800 | tf_op jit(solution)/shard_map/reshape | solution.py:96
  159.8 5.0 %copy.70 = bf16[2,1280,5,64]{3,0,2,1:T(2,128)(2,1)} copy(bf16[2,1280,5,64]{1,3,2,0:T(8,128)(2,1)S(1)} %bitcast.210) | data formatting | bytes 3276800 | tf_op jit(solution)/shard_map/reshape | solution.py:94
  164.9 5.1 %copy.71 = bf16[2,1280,5,64]{3,0,2,1:T(2,128)(2,1)} copy(bf16[2,1280,5,64]{1,3,2,0:T(8,128)(2,1)S(1)} %bitcast.209) | data formatting | bytes 3276800 | tf_op jit(solution)/shard_map/reshape | solution.py:95
  170.0 10.3 %fusion.157 = f32[1280,5,2,2]{2,3,1,0:T(2,128)} fusion(bf16[2,1280,5,64]{3,0,2,1:T(2,128)(2,1)} %copy.70, bf16[2,1280,5,64]{3,0,2,1:T(2,128)(2,1)} %copy.71), kind=kOutput, calls=%fused_computation.195 | convolution fusion | flops 3276800 | bytes 3379200 | tf_op jit(solution)/shard_map/fnhd,gnhd->nhfg/dot_general | solution.py:101
  180.2 7.1 %copy.72 = f32[1280,5,2,2]{0,3,2,1:T(2,128)S(1)} copy(f32[1280,5,2,2]{2,3,1,0:T(2,128)} %fusion.157) | data formatting | bytes 204800 | tf_op jit(solution)/shard_map/fnhd,gnhd->nhfg/dot_general | solution.py:101
  188.2 119.7 %all-reduce.7.cloned.1.call-done = bf16[8,1280,320]{1,0,2:T(8,128)(2,1)} async-done(((bf16[8,1280,320]{1,0,2:T(8,128)(2,1)}), bf16[8,1280,320]{1,0,2:T(8,128)(2,1)}) %all-reduce.7.cloned.1.call-update) | async-done | bytes 6553616 | tf_op jit(solution)/shard_map/psum | solution.py:167
  308.0 9.5 %convolution_convert_fusion = bf16[8,1280,640]{1,2,0:T(8,128)(2,1)S(1)} fusion(bf16[8,1280,320]{1,0,2:T(8,128)(2,1)} %all-reduce.7.cloned.1.call-done, bf16[320,960]{1,0:T(8,128)(2,1)S(1)} %copy-done.13), kind=kOutput, calls=%fused_computation | convolution fusion | flops 4200857600 | bytes 20070400 | tf_op jit(solution)/shard_map/dot_general | solution.py:168
  317.4 4.9 %fusion.152 = (bf16[8,1280,320]{1,2,0:T(8,128)(2,1)}, bf16[8,1280,320]{1,2,0:T(8,128)(2,1)}) fusion(bf16[8,1280,640]{1,2,0:T(8,128)(2,1)S(1)} %convolution_convert_fusion), kind=kLoop, calls=%fused_computation.190 | loop fusion | bytes 26214400 | tf_op jit(solution)/shard_map/slice | solution.py:98
  322.3 18.5 %copy.76 = bf16[8,1280,5,64]{3,0,2,1:T(8,128)(2,1)} copy(bf16[8,1280,5,64]{1,3,2,0:T(8,128)(2,1)} %bitcast.205) | data formatting | bytes 13107200 | tf_op jit(solution)/shard_map/reshape | solution.py:97
  340.8 15.6 %fusion.156 = (f32[1280,5,2]{2,1,0:T(8,128)}, f32[1280,5,2,8]{3,2,1,0:T(2,128)}) fusion(bf16[2,1280,5,64]{3,0,2,1:T(2,128)(2,1)S(1)} %copy-done.6, bf16[8,1280,5,64]{3,0,2,1:T(8,128)(2,1)} %copy.76), kind=kOutput, calls=%fused_computation.194 | convolution fusion | flops 13299200 | bytes 8652800 | tf_op jit(solution)/shard_map/fnhd,jnhd->nhfj/dot_general | solution.py:107
  363.0 19.2 %fusion.28 = f32[1280,5,2]{2,1,0:T(8,128)} fusion(f32[1280,5,2,8]{3,2,1,0:T(2,128)} %get-tuple-element.40, f32[1280,5,2]{2,1,0:T(8,128)} %copy.78), kind=kLoop, calls=%fused_computation.51 | loop fusion | flops 192000 | bytes 512000 | tf_op jit(solution)/shard_map/reduce_sum | solution.py:113
  388.7 5.1 %copy.81 = bf16[1280,5,2,2]{3,2,1,0:T(2,128)(2,1)} copy(bf16[1280,5,2,2]{0,3,2,1:T(2,128)(2,1)S(1)} %divide_convert_fusion.2) | data formatting | bytes 102400 | tf_op jit(solution)/shard_map/convert_element_type | solution.py:116
  393.8 18.2 %copy.83 = bf16[8,1280,5,64]{3,0,2,1:T(8,128)(2,1)} copy(bf16[8,1280,5,64]{1,3,2,0:T(8,128)(2,1)} %bitcast.204) | data formatting | bytes 13107200 | tf_op jit(solution)/shard_map/reshape | solution.py:98
  412.0 11.1 %fusion.158 = f32[1280,5,64,2]{2,3,1,0:T(2,128)} fusion(bf16[2,1280,5,64]{3,0,2,1:T(2,128)(2,1)} %copy.80, bf16[1280,5,2,2]{3,2,1,0:T(2,128)(2,1)} %copy.81), kind=kOutput, calls=%fused_computation.196 | convolution fusion | flops 3276800 | bytes 4966400 | tf_op jit(solution)/shard_map/nhfg,gnhd->fnhd/dot_general | solution.py:118
  423.1 20.5 %fusion.2 = bf16[2,1280,5,64]{3,0,2,1:T(2,128)(2,1)} fusion(f32[1280,5,64,2]{2,3,1,0:T(2,128)} %fusion.158, bf16[8,1280,5,64]{3,0,2,1:T(8,128)(2,1)S(1)} %copy-done.3, f32[1280,5,2,8]{3,2,1,0:T(2,128)} %get-tuple-element.40, f32[1280,5,2]{2,1,0:T(8,128)} %copy.82, f32[1280,5,2]{2,1,0:T(8,128)S(1)} %bitcast.207), kind=kOutput, calls=%fused_computation.21 | convolution fusion | flops 15052800 | bytes 11980800 | tf_op jit(solution)/shard_map/nhfj,jnhd->fnhd/dot_general | solution.py:121
  443.6 6.1 %copy.84 = bf16[2,1280,5,64]{1,3,2,0:T(8,128)(2,1)S(1)} copy(bf16[2,1280,5,64]{3,0,2,1:T(2,128)(2,1)} %fusion.2) | data formatting | bytes 3276800 | tf_op jit(solution)/shard_map/convert_element_type | solution.py:124
  (121 shorter events, 109.2 us)
Async XLA Ops:
  6.5 443.2 %copy-start = (bf16[320,320]{1,0:T(8,128)(2,1)S(1)}, bf16[320,320]{1,0:T(8,128)(2,1)}, u32[]{:S(2)}) copy-start(bf16[320,320]{1,0:T(8,128)(2,1)} %param.21) | copy-start | bytes 614404
  6.5 301.4 %all-reduce.7.cloned.1.call-start = ((), (), s32[]{:S(2)}) async-start(), calls=%async_computation | async-start | bytes 13107200 | tf_op jit(solution)/shard_map/psum | solution.py:167
  18.8 10.7 %collective-permute-start.1 = (bf16[2,1,64,320]{3,2,1,0:T(8,128)(2,1)S(1)}, bf16[2,1,64,320]{3,2,1,0:T(8,128)(2,1)S(1)}, u32[]{:S(2)}, u32[]{:S(2)}) collective-permute-start(bf16[2,1,64,320]{3,2,1,0:T(8,128)(2,1)S(1)} %get-tuple-element.29), channel_id=1, source_target_pairs={{1,0},{3,2},{5,4},{7,6},{9,8},{11,10},{13,12},{15,14},{17,16},{19,... | collective-permute-start | bytes 245768 | tf_op jit(solution)/shard_map/ppermute | solution.py:24
  20.1 9.4 %collective-permute-start = (bf16[2,1,64,320]{3,2,1,0:T(8,128)(2,1)S(1)}, bf16[2,1,64,320]{3,2,1,0:T(8,128)(2,1)S(1)}, u32[]{:S(2)}, u32[]{:S(2)}) collective-permute-start(bf16[2,1,64,320]{3,2,1,0:T(8,128)(2,1)S(1)} %get-tuple-element.28), channel_id=1, source_target_pairs={{0,1},{2,3},{4,5},{6,7},{8,9},{10,11},{12,13},{14,15},{16,17},{18,... | collective-permute-start | bytes 245768 | tf_op jit(solution)/shard_map/ppermute | solution.py:21
  48.9 3.3 copy-start.2
  52.2 15.2 %copy-start.16 = (f32[320]{0:T(512)S(1)}, f32[320]{0:T(512)}, u32[]{:S(2)}) copy-start(f32[320]{0:T(512)} %param.16) | copy-start | bytes 3844
  67.4 7.1 %copy-start.10 = (bf16[3,3,320,320]{3,2,1,0:T(8,128)(2,1)S(1)}, bf16[3,3,320,320]{3,2,1,0:T(8,128)(2,1)}, u32[]{:S(2)}) copy-start(bf16[3,3,320,320]{3,2,1,0:T(8,128)(2,1)} %param.17) | copy-start | bytes 5529604
  68.6 9.2 %collective-permute-start.3 = (bf16[2,1,64,320]{3,2,1,0:T(8,128)(2,1)S(1)}, bf16[2,1,64,320]{3,2,1,0:T(8,128)(2,1)S(1)}, u32[]{:S(2)}, u32[]{:S(2)}) collective-permute-start(bf16[2,1,64,320]{3,2,1,0:T(8,128)(2,1)S(1)} %get-tuple-element.27), channel_id=1, source_target_pairs={{1,0},{3,2},{5,4},{7,6},{9,8},{11,10},{13,12},{15,14},{17,16},{19,... | collective-permute-start | bytes 245768 | tf_op jit(solution)/shard_map/ppermute | solution.py:24
  69.9 7.9 %collective-permute-start.2 = (bf16[2,1,64,320]{3,2,1,0:T(8,128)(2,1)S(1)}, bf16[2,1,64,320]{3,2,1,0:T(8,128)(2,1)S(1)}, u32[]{:S(2)}, u32[]{:S(2)}) collective-permute-start(bf16[2,1,64,320]{3,2,1,0:T(8,128)(2,1)S(1)} %get-tuple-element.26), channel_id=1, source_target_pairs={{0,1},{2,3},{4,5},{6,7},{8,9},{10,11},{12,13},{14,15},{16,17},{18,... | collective-permute-start | bytes 245768 | tf_op jit(solution)/shard_map/ppermute | solution.py:21
  99.1 3.4 copy-start.1
  117.3 6.2 %collective-permute-start.4 = (bf16[20,64,320]{2,1,0:T(8,128)(2,1)}, bf16[20,64,320]{2,1,0:T(8,128)(2,1)}, u32[]{:S(2)}, u32[]{:S(2)}) collective-permute-start(bf16[20,64,320]{2,1,0:T(8,128)(2,1)} %get-tuple-element.25), channel_id=1, source_target_pairs={{0,2},{2,4},{4,6},{6,8},{8,10},{10,12},{12,14},{14,16},{16,18},{18... | collective-permute-start | bytes 2457608 | tf_op jit(solution)/shard_map/ppermute | solution.py:32
  119.7 3.8 copy-start.5
  119.7 3.8 copy-start.11
  119.7 6.5 %collective-permute-start.5 = (bf16[20,64,320]{2,1,0:T(8,128)(2,1)}, bf16[20,64,320]{2,1,0:T(8,128)(2,1)S(1)}, u32[]{:S(2)}, u32[]{:S(2)}) collective-permute-start(bf16[20,64,320]{2,1,0:T(8,128)(2,1)} %get-tuple-element.22), channel_id=1, source_target_pairs={{2,0},{4,2},{6,4},{8,6},{10,8},{12,10},{14,12},{16,14},{18,16},{20... | collective-permute-start | bytes 2457608 | tf_op jit(solution)/shard_map/ppermute | solution.py:32
  126.3 3.3 copy-start.15
  129.6 8.5 %copy-start.17 = (s32[8]{0:T(128)S(1)}, s32[8]{0:T(128)}, u32[]{:S(2)}) copy-start(s32[8]{0:T(128)} %param.13) | copy-start | bytes 100
  180.2 127.7 %copy-start.13 = (bf16[320,960]{1,0:T(8,128)(2,1)S(1)}, bf16[320,960]{1,0:T(8,128)(2,1)}, u32[]{:S(2)}) copy-start(bf16[320,960]{1,0:T(8,128)(2,1)} %param.20) | copy-start | bytes 1843204
  187.4 130.0 %copy-start.7 = (f32[1280,5,2,2]{0,3,2,1:T(2,128)}, f32[1280,5,2,2]{0,3,2,1:T(2,128)S(1)}, u32[]{:S(2)}) copy-start(f32[1280,5,2,2]{0,3,2,1:T(2,128)S(1)} %copy.72) | copy-start | bytes 307204
  322.3 18.5 %copy-start.6 = (bf16[2,1280,5,64]{3,0,2,1:T(2,128)(2,1)S(1)}, bf16[2,1280,5,64]{3,0,2,1:T(2,128)(2,1)}, u32[]{:S(2)}) copy-start(bf16[2,1280,5,64]{3,0,2,1:T(2,128)(2,1)} %copy.70) | copy-start | bytes 4915204
  356.5 3.1 copy-start.14
  356.5 3.1 copy-start.8
  393.8 29.3 %slice-start = ((s8[5242880]{0:T(1024)(128)(4,1)}), s8[1048576]{0:T(1024)(128)(4,1)S(1)}, s32[]{:S(2)}) async-start(s8[5242880]{0:T(1024)(128)(4,1)} %bitcast.206), calls=%async_computation.1 | async-start | bytes 2097152
  412.0 11.1 %slice-start.1 = ((s8[5242880]{0:T(1024)(128)(4,1)}), s8[4194304]{0:T(1024)(128)(4,1)S(1)}, s32[]{:S(2)}) async-start(s8[5242880]{0:T(1024)(128)(4,1)} %bitcast.206), calls=%async_computation.2 | async-start | bytes 8388608
  412.0 11.1 %copy-start.3 = (bf16[8,1280,5,64]{3,0,2,1:T(8,128)(2,1)S(1)}, bf16[8,1280,5,64]{3,0,2,1:T(8,128)(2,1)}, u32[]{:S(2)}) copy-start(bf16[8,1280,5,64]{3,0,2,1:T(8,128)(2,1)} %copy.83) | copy-start | bytes 19660804
  (3 other events, 7.1 us)
Sparse Core Ops, SparseCore 0:
  144.0 163.9 all-reduce.6
where the time goes:
time: 468 us; the launch traced here: 462 us
  matrix products  161 us (34%)
  waiting for transfers between devices  120 us (26%)
  local copies, waits for them, and re-layouts  107 us (23%)
  other arithmetic  33.6 us (7%)
  starting transfers between devices  15.5 us (3%)
  between operations  14.8 us (3%)
  blocking collectives  10.8 us (2%)
    psum x1, waiting for transfers between devices, local(): picked = lax.psum(picked.astype(jnp.bfloat16), 'clip')  120 us
    dot_general x18, matrix products, convolve(): jnp.dot(window, weights[row_step, col_step], preferred_element_type=jnp.f...  74 us
    dot_general x1, matrix products, attend(): jnp.einsum('nhfj,jnhd->fnhd', far_weight, values_shared, preferred_elemen...  20.5 us
    reduce_sum x1, other arithmetic, attend(): jnp.sum(far_exp, axis=-1, keepdims=True)  19.2 us
    reshape x1, local copies, waits for them, and re-layouts, attend(): keys_shared = shared_kv[..., :channels].reshape(shape_shared)  18.5 us
    reshape x1, local copies, waits for them, and re-layouts, attend(): values_shared = shared_kv[..., channels:].reshape(shape_shared)  18.2 us
    dot_general x1, matrix products, attend(): jnp.einsum('fnhd,jnhd->nhfj', queries, keys_shared, preferred_element_typ...  15.6 us
    dot_general x1, matrix products, attend(): jnp.einsum('nhfg,gnhd->fnhd', near_weight, values_local, preferred_elemen...  11.1 us
  transfers between devices with their start and end apart: 7, of which 1 were waited for; matrix products, arithmetic and copies ran while one was open for 12% of the time, Pallas kernels for 0%

commit v1 on v0

v1 whole, which is shorter than its diff:
```python
import functools

import jax
import jax.numpy as jnp
from jax import lax
from jax.experimental import pallas as pl
from jax.experimental.pallas import tpu as pltpu
from jax.sharding import PartitionSpec as P

HEAD_DIM = 64
GROUPS = 32
H = 40
W = 64
EPS = 1e-05
MASKED = -1e30
LANES = 128
FLAG_ROWS = 16
F32 = jnp.float32
BF16 = jnp.bfloat16
VMEM_LIMIT = 48 * 1024 * 1024

SMEM = pl.BlockSpec(memory_space=pltpu.SMEM)
VMEM = pl.BlockSpec(memory_space=pltpu.VMEM)
ANY = pl.BlockSpec(memory_space=pl.ANY)


def call(kernel, out_shape, in_specs, args, scratch=(), flops=0, name=None):
    moved = sum(a.size * a.dtype.itemsize for a in args)
    moved += sum(o.size * o.dtype.itemsize for o in out_shape)
    return pl.pallas_call(
        kernel,
        out_shape=out_shape,
        in_specs=in_specs,
        out_specs=[VMEM] * len(out_shape),
        scratch_shapes=list(scratch),
        compiler_params=pltpu.CompilerParams(vmem_limit_bytes=VMEM_LIMIT),
        cost_estimate=pl.CostEstimate(flops=flops, bytes_accessed=moved, transcendentals=0),
        name=name,
    )(*args)


def struct(shape, dtype=BF16):
    return jax.ShapeDtypeStruct(shape, dtype)


def silu(x):
    return 0.5 * x * (1.0 + jnp.tanh(0.5 * x))


def column_sums(v):
    folded = v.reshape(v.shape[0] // 8, 8, v.shape[1])
    return jnp.sum(folded, axis=0), jnp.sum(folded * folded, axis=0)


def split3(x):
    high = x.astype(BF16)
    rest = x - high.astype(F32)
    mid = rest.astype(BF16)
    return high, mid, (rest - mid.astype(F32)).astype(BF16)


def put_stats(f, sums, stats_ref, msg_ref, cols):
    channels = sums.shape[1]
    stats_ref[f] = jnp.concatenate([sums, jnp.zeros((6, channels), F32)], axis=0)
    high, mid, low = split3(sums)
    parts = [high, mid, low, jnp.zeros((FLAG_ROWS - 6, channels), BF16)]
    packed = jnp.concatenate([p.astype(F32) for p in parts], axis=0)
    msg_ref[f, pl.ds(cols, FLAG_ROWS), :] = packed.astype(BF16)


def stats_kernel(cols, scalars, x_ref, stats_ref, msg_ref):
    frames, cells, channels = x_ref.shape
    step = 2 * cols if cells % (2 * cols) == 0 else cols
    for f in range(frames):

        def body(i, carry):
            v = x_ref[f, pl.ds(pl.multiple_of(i * step, step), step), :].astype(F32)
            s, q = column_sums(v)
            return carry[0] + s, carry[1] + q

        zero = jnp.zeros((8, channels), F32)
        s, q = lax.fori_loop(0, cells // step, body, (zero, zero))
        sums = jnp.concatenate(
            [jnp.sum(s, axis=0, keepdims=True), jnp.sum(q, axis=0, keepdims=True)], axis=0
        )
        put_stats(f, sums, stats_ref, msg_ref, cols)
        edge = pl.multiple_of(scalars[2], cols)
        msg_ref[f, pl.ds(0, cols), :] = x_ref[f, pl.ds(edge, cols), :]


def arrange(pieces):
    big = pieces[0].shape[1] // 256 * 256
    return jnp.concatenate([p[:, :big] for p in pieces] + [p[:, big:] for p in pieces], axis=1)


def place(total, w, index, count, channels, by_rows):
    pass


def conv_kernel(cols, total_cells, residual, scalars, x_ref, stats_ref, top_ref, bottom_ref, gain_ref, w_ref, *rest):
    if residual:
        (res_in_ref, res_ref, move_ref, one_ref, two_ref, wide_w, wide_x, wide_y) = rest
    else:
        (out_ref, out_stats_ref, msg_ref, wide_w, wide_x, wide_y) = rest
    frames, cells, channels = x_ref.shape
    big = channels // 256 * 256
    small = channels - big

    def spans(index):
        return ((index * big, big, 0), (3 * big + index * small, small, big))

    for a in range(3):
        for b in range(3):
            w = w_ref[3 * a + b]
            for row, height, from_row in spans(b):
                for col, width, from_col in spans(a):
                    wide_w[row : row + height, col : col + width] = w[
                        from_row : from_row + height, from_col : from_col + width
                    ]

    group_width = channels // GROUPS
    row_group = lax.broadcasted_iota(jnp.int32, (channels, channels), 0) // group_width
    col_group = lax.broadcasted_iota(jnp.int32, (channels, channels), 1) // group_width
    same = (row_group == col_group).astype(F32)
    step = cols * (4 if cells % (4 * cols) == 0 else 1)
    padded = cells + 2 * cols
    mm = padded // 4

    for f in range(frames):
        other = top_ref[f, pl.ds(cols, FLAG_ROWS), :].astype(F32)
        sums = stats_ref[f, 0:2, :] + other[0:2] + other[2:4] + other[4:6]
        sums = jnp.concatenate([sums, jnp.zeros((6, channels), F32)], axis=0)
        means = jnp.dot(
            sums, same, preferred_element_type=F32, precision=lax.Precision.HIGHEST
        ) / (total_cells * group_width)
        centre = means[0:1]
        inverse = lax.rsqrt(means[1:2] - centre * centre + EPS)
        scale = inverse * gain_ref[...]
        shift = -centre * scale

        def widen(raw, keep):
            length = raw.shape[0]
            y = silu(raw.astype(F32) * scale + shift)
            if keep is not None:
                y = jnp.where(keep, y, 0.0)
            column = lax.broadcasted_iota(jnp.int32, (length, 1), 0) % cols
            left = jnp.where(column == 0, 0.0, pltpu.roll(y, 1, 0))
            right = jnp.where(column == cols - 1, 0.0, pltpu.roll(y, length - 1, 0))
            return arrange([left, y, right]).astype(BF16)

        wide_x[0:cols] = widen(top_ref[f, 0:cols, :], scalars[0] > 0)
        wide_x[cells + cols : cells + 2 * cols] = widen(bottom_ref[f, 0:cols, :], scalars[1] > 0)

        def act_body(i, carry):
            start = pl.multiple_of(i * step, step)
            wide_x[pl.ds(start + cols, step), :] = widen(x_ref[f, pl.ds(start, step), :], None)
            return carry

        lax.fori_loop(0, cells // step, act_body, 0)

        def dot_body(i, carry):
            start = pl.multiple_of(i * mm, mm)
            wide_y[pl.ds(start, mm), :] = jnp.dot(
                wide_x[pl.ds(start, mm), :], wide_w[...], preferred_element_type=F32
            )
            return carry

        lax.fori_loop(0, padded // mm, dot_body, 0)

        def sum_rows(start):
            parts = []
            for base, width in ((0, big), (3 * big, small)):
                total = wide_y[pl.ds(start, step), base : base + width]
                total = total + wide_y[pl.ds(start + cols, step), base + width : base + 2 * width]
                total = total + wide_y[pl.ds(start + 2 * cols, step), base + 2 * width : base + 3 * width]
                parts.append(total)
            return jnp.concatenate(parts, axis=1)

        if residual:
            last = scalars[3] - 1
            odd = scalars[4] > 0

            def end_body(i, carry):
                start = pl.multiple_of(i * step, step)
                here = pl.ds(start, step)
                total = (res_in_ref[f, here, :].astype(F32) + sum_rows(start)).astype(BF16)
                res_ref[f, here, :] = total
                moving = silu(total.astype(F32)).astype(BF16)
                move_ref[f, here, :] = moving
                for ref, final in ((one_ref, jnp.logical_not(odd)), (two_ref, odd)):

                    @pl.when(jnp.where(final, f == last, f == 0))
                    def _():
                        ref[here, :] = moving

                return carry

            lax.fori_loop(0, cells // step, end_body, 0)
        else:

            def end_body(i, carry):
                start = pl.multiple_of(i * step, step)
                total = sum_rows(start).astype(BF16)
                out_ref[f, pl.ds(start, step), :] = total
                s, q = column_sums(total.astype(F32))
                return carry[0] + s, carry[1] + q

            zero = jnp.zeros((8, channels), F32)
            s, q = lax.fori_loop(0, cells // step, end_body, (zero, zero))
            sums = jnp.concatenate(
                [jnp.sum(s, axis=0, keepdims=True), jnp.sum(q, axis=0, keepdims=True)], axis=0
            )
            put_stats(f, sums, out_stats_ref, msg_ref, cols)
            edge = pl.multiple_of(scalars[2], cols)
            msg_ref[f, pl.ds(0, cols), :] = out_ref[f, pl.ds(edge, cols), :]


def time_kernel(group, scalars, res_ref, move_ref, one_ref, two_ref, w_ref, gain_ref, *rest):
    res_two_ref, shares, wide_w = rest[0], rest[1 : 1 + group], rest[1 + group]
    frames, cells, channels = res_ref.shape
    big = channels // 256 * 256
    small = channels - big
    share = cells // group
    live = scalars[3]
    odd = scalars[4] > 0
    for a in range(3):
        w = w_ref[a]
        wide_w[a * big : (a + 1) * big, :] = w[:big]
        wide_w[3 * big + a * small : 3 * big + (a + 1) * small, :] = w[big:]
    for d in range(group):
        start = pl.multiple_of(scalars[8 + d] * share, 16)
        here = pl.ds(start, share)
        one = one_ref[here, :].astype(F32)
        two = two_ref[here, :].astype(F32)
        prior = jnp.where(odd, one, two)
        later = jnp.where(odd, two, one)
        moving = [move_ref[f, here, :].astype(F32) for f in range(frames)]
        for f in range(frames):
            before = moving[f - 1] if f else prior
            after = moving[f + 1] if f + 1 < frames else jnp.zeros_like(prior)
            after = jnp.where(live == f + 1, later, after)
            x = arrange([before, moving[f], after]).astype(BF16)
            mixed = res_ref[f, here, :].astype(F32) + jnp.dot(
                x, wide_w[...], preferred_element_type=F32
            )
            res_two = mixed.astype(BF16)
            res_two_ref[f, here, :] = res_two
            v = res_two.astype(F32)
            centre = jnp.mean(v, axis=1, keepdims=True)
            v = v - centre
            spread = jnp.mean(v * v, axis=1, keepdims=True)
            normed = v * lax.rsqrt(spread + EPS) * gain_ref[...]
            shares[d][f, pl.ds(0, share), :] = normed.astype(BF16)
            flag = jnp.where(f < live, 1.0, 0.0)
            shares[d][f, pl.ds(share, FLAG_ROWS), :] = jnp.full(
                (FLAG_ROWS, channels), flag, F32
            ).astype(BF16)


def attend_kernel(group, buffers, contexts, scalars, *rest):
    own = rest[:group]
    sources = rest[group : group + buffers]
    w_ref = rest[group + buffers]
    outs = rest[group + buffers + 1 : 2 * group + buffers + 1]
    wide_w, context, packed, shared, sems = rest[2 * group + buffers + 1 :]
    frames, flagged, channels = own[0].shape
    share = flagged - FLAG_ROWS
    heads = channels // HEAD_DIM
    wide = (channels + LANES - 1) // LANES * LANES
    keys = frames + contexts

    for j in range(contexts):
        for b in range(buffers):

            @pl.when(scalars[8 + group + 2 * j] == b)
            def _():
                pltpu.make_async_copy(
                    sources[b].at[scalars[9 + group + 2 * j]], context.at[j], sems.at[j]
                ).start()

    wide_w[...] = jnp.zeros_like(wide_w)
    for part in range(3):
        wide_w[:, part * wide : part * wide + channels] = w_ref[:, part * channels : (part + 1) * channels]
    for d in range(group):
        for f in range(frames):
            packed[d, f] = jnp.dot(
                own[d][f, 0:share, :], wide_w[...], preferred_element_type=F32
            ).astype(BF16)
    for j in range(contexts):
        pltpu.make_async_copy(sources[0].at[0], context.at[j], sems.at[j]).wait()
    for j in range(contexts):
        shared[j] = jnp.dot(
            context[j], wide_w[:, wide:], preferred_element_type=F32
        ).astype(BF16)

    gather_row = lax.broadcasted_iota(jnp.int32, (keys * wide, LANES), 0)
    gather_lane = lax.broadcasted_iota(jnp.int32, (keys * wide, LANES), 1)
    gather = (gather_row // wide * 8 + gather_row % wide // HEAD_DIM == gather_lane).astype(F32)
    gather = (gather * HEAD_DIM ** (-0.5)).astype(BF16)
    spread_row = lax.broadcasted_iota(jnp.int32, (LANES, keys * wide), 0)
    spread_col = lax.broadcasted_iota(jnp.int32, (LANES, keys * wide), 1)
    spread = (spread_col // wide * 8 + spread_col % wide // HEAD_DIM == spread_row).astype(BF16)
    lane = lax.broadcasted_iota(jnp.int32, (1, LANES), 1)
    step = 80 if share % 80 == 0 else share
    for d in range(group):
        flags = own[d][:, pl.ds(share, FLAG_ROWS), 0:LANES].astype(F32)
        visible = jnp.logical_and(lane % 8 < heads, lane // 8 < keys)
        for f in range(frames):
            dead = jnp.logical_and(lane // 8 == f, flags[f, 0:1] < 0.5)
            visible = jnp.logical_and(visible, jnp.logical_not(dead))

        def body(i, carry, d=d, visible=visible):
            here = pl.ds(pl.multiple_of(i * step, 16), step)
            key = [packed[d, f, here, wide : 2 * wide] for f in range(frames)]
            key += [shared[j, here, 0:wide] for j in range(contexts)]
            value = [packed[d, f, here, 2 * wide : 3 * wide] for f in range(frames)]
            value += [shared[j, here, wide : 2 * wide] for j in range(contexts)]
            for f in range(frames):
                query = packed[d, f, here, 0:wide]
                products = jnp.concatenate([query * k for k in key], axis=1)
                scores = jnp.dot(products, gather, preferred_element_type=F32)
                scores = jnp.where(visible, scores, MASKED)
                top = scores
                for shift in (8, 16, 32, 64):
                    top = jnp.maximum(top, pltpu.roll(top, shift, 1))
                raised = jnp.exp(scores - top)
                total = raised
                for shift in (8, 16, 32, 64):
                    total = total + pltpu.roll(total, shift, 1)
                weights = (raised / total).astype(BF16)
                wide_weights = jnp.dot(weights, spread, preferred_element_type=F32)
                result = jnp.zeros((step, wide), F32)
                for j in range(keys):
                    result = result + wide_weights[:, j * wide : (j + 1) * wide] * value[j].astype(F32)
                outs[d][f, here, :] = result[:, :channels].astype(BF16)
            return carry

        lax.fori_loop(0, share // step, body, 0)


def final_kernel(group, scalars, res_ref, *rest):
    parts, w_ref, out_ref = rest[:group], rest[group], rest[group + 1]
    frames, cells, channels = res_ref.shape
    share = cells // group
    for d in range(group):
        here = pl.ds(pl.multiple_of(scalars[8 + d] * share, 16), share)
        for f in range(frames):
            total = res_ref[f, here, :].astype(F32) + jnp.dot(
                parts[d][f], w_ref[...], preferred_element_type=F32
            )
            out_ref[f, here, :] = jnp.where(f < scalars[3], total, 0.0).astype(BF16)


def share_tile(stats, msg, source, cols):
    tiles = lax.axis_size("tile")
    if tiles == 2:
        got = lax.ppermute(msg, "tile", [(0, 1), (1, 0)])
        return stats, got, got
    down = [(i, i + 1) for i in range(tiles - 1)]
    up = [(i + 1, i) for i in range(tiles - 1)]
    pad = ((0, 0), (0, FLAG_ROWS), (0, 0))
    top = lax.ppermute(source[:, -cols:], "tile", down)
    bottom = lax.ppermute(source[:, :cols], "tile", up)
    return lax.psum(stats, "tile"), jnp.pad(top, pad), jnp.pad(bottom, pad)


def local(
    latents,
    lengths,
    context,
    gain_first,
    conv_first,
    gain_second,
    conv_second,
    time_weight,
    attn_gain,
    w_qkv,
    w_out,
):
    frames, rows, cols, channels = latents.shape
    cells = rows * cols
    tiles, clips = lax.axis_size("tile"), lax.axis_size("clip")
    tile, clip = lax.axis_index("tile"), lax.axis_index("clip")
    group = 4
    levels = clips // group
    share = cells // group
    contexts = context.shape[0]
    member, level = clip % group, clip // group
    total_cells = cells * tiles

    owner = context // frames
    source_level = owner // group
    hop = level - source_level
    buffer = jnp.where(hop >= 0, hop, levels - 1 - hop)
    slot = (owner % group) ^ member
    scalars = jnp.concatenate(
        [
            jnp.stack(
                [
                    (tile > 0).astype(jnp.int32),
                    (tile < tiles - 1).astype(jnp.int32),
                    jnp.where(tile == 0, cells - cols, 0).astype(jnp.int32),
                    lengths[0],
                    clip % 2,
                    clip * 0,
                    clip * 0,
                    clip * 0,
                ]
            ),
            member ^ jnp.arange(group, dtype=jnp.int32),
            jnp.stack([buffer, slot], axis=1).reshape(-1),
        ]
    ).astype(jnp.int32)

    x = latents.reshape(frames, cells, channels)
    message = struct((frames, cols + FLAG_ROWS, channels))
    sums = struct((frames, 8, channels), F32)
    whole = struct((frames, cells, channels))
    stats, msg = call(
        functools.partial(stats_kernel, cols), [sums, message], [SMEM, VMEM], [scalars, x], name="first_sums"
    )

    conv_scratch = [
        pltpu.VMEM((3 * channels, 3 * channels), BF16),
        pltpu.VMEM((cells + 2 * cols, 3 * channels), BF16),
        pltpu.VMEM((cells + 2 * cols, 3 * channels), F32),
    ]
    conv_flops = 2 * frames * cells * 9 * channels * channels
    stats, top, bottom = share_tile(stats, msg, x, cols)
    hidden, stats, msg = call(
        functools.partial(conv_kernel, cols, total_cells, False),
        [whole, sums, message],
        [SMEM] + [VMEM] * 6,
        [scalars, x, stats, top, bottom, gain_first.reshape(1, channels), conv_first.reshape(9, channels, channels)],
        conv_scratch,
        conv_flops,
        name="conv_one",
    )
    stats, top, bottom = share_tile(stats, msg, hidden, cols)
    one_frame = struct((cells, channels))
    res_one, moving, one, two = call(
        functools.partial(conv_kernel, cols, total_cells, True),
        [whole, whole, one_frame, one_frame],
        [SMEM] + [VMEM] * 7,
        [scalars, hidden, stats, top, bottom, gain_second.reshape(1, channels), conv_second.reshape(9, channels, channels), x],
        conv_scratch,
        conv_flops,
        name="conv_two",
    )
    one = lax.ppermute(one, "clip", [(i, i ^ 1) for i in range(clips)])
    two = lax.ppermute(
        two, "clip", [(i, i + 1) for i in range(1, clips - 1, 2)] + [(i + 1, i) for i in range(1, clips - 1, 2)]
    )
    part = struct((frames, share + FLAG_ROWS, channels))
    res_two, *shares = call(
        functools.partial(time_kernel, group),
        [whole] + [part] * group,
        [SMEM] + [VMEM] * 6,
        [scalars, res_one, moving, one, two, time_weight, attn_gain.reshape(1, channels)],
        [pltpu.VMEM((3 * channels, channels), BF16)],
        2 * frames * cells * 3 * channels * channels,
        name="time_mix",
    )
    swaps = [[(i, i ^ d) for i in range(clips)] for d in range(group)]
    own = [shares[0]] + [lax.ppermute(shares[d], "clip", swaps[d]) for d in range(1, group)]

    picks = []
    for d in range(group):
        other = clip ^ d
        second = jnp.any(context == other * frames + 1)
        picks.append(jnp.where(second, own[d][1, :share], own[d][0, :share]))
    picked = jnp.stack(picks)
    rising = [(i, i + group) for i in range(clips - group)]
    falling = [(i + group, i) for i in range(clips - group)]
    below, above = [picked], [picked]
    for _ in range(levels - 1):
        below.append(lax.ppermute(below[-1], "clip", rising))
        above.append(lax.ppermute(above[-1], "clip", falling))
    sources = below + above[1:]

    wide = (channels + LANES - 1) // LANES * LANES
    attended = call(
        functools.partial(attend_kernel, group, len(sources), contexts),
        [struct((frames, share, channels))] * group,
        [SMEM] + [VMEM] * group + [ANY] * len(sources) + [VMEM],
        [scalars, *own, *sources, w_qkv],
        [
            pltpu.VMEM((channels, 3 * wide), BF16),
            pltpu.VMEM((contexts, share, channels), BF16),
            pltpu.VMEM((group, frames, share, 3 * wide), BF16),
            pltpu.VMEM((contexts, share, 2 * wide), BF16),
            pltpu.SemaphoreType.DMA((contexts,)),
        ],
        2 * frames * cells * channels * 10 * channels,
        name="attend",
    )
    parts = [attended[0]] + [lax.ppermute(attended[d], "clip", swaps[d]) for d in range(1, group)]
    (result,) = call(
        functools.partial(final_kernel, group),
        [whole],
        [SMEM] + [VMEM] * (group + 2),
        [scalars, res_two, *parts, w_out],
        flops=2 * frames * cells * channels * channels,
        name="project",
    )
    return result.reshape(frames, rows, cols, channels)


def solution(mesh):
    placed = (P("clip", "tile", None, None), P("clip"), P(), P(), P(), P(), P(), P(), P(), P(), P())
    return jax.shard_map(
        local, mesh=mesh, in_specs=placed, out_specs=P("clip", "tile", None, None), check_vma=False
    )
```

time: 468 us -> 263 us (0.56); the launches traced: 462 us -> 263 us
  matrix products: 161 us -> 0 us
  local copies, waits for them, and re-layouts: 107 us -> 13 us
  Pallas kernels: 0 us -> 88.9 us
  starting transfers between devices: 15.5 us -> 46 us
  other arithmetic: 33.6 us -> 4.33 us
  between operations: 14.8 us -> 1 us
  waiting for transfers between devices: 120 us -> 109 us
  blocking collectives: 10.8 us -> 0 us
    dot_general x29 -> x0, matrix products: 161 us -> none  [the longest x18 74 us: convolve(): jnp.dot(window, weights[row_step, col_step], preferred_element_type=jnp.f...]
    psum x1 -> x0, waiting for transfers between devices: 120 us -> none  [local(): picked = lax.psum(picked.astype(jnp.bfloat16), 'clip')]
    ppermute x6 -> x16, waiting for transfers between devices: 0.02 us -> 109 us  [the longest x3 56.9 us: local(): above.append(lax.ppermute(above[-1], 'clip', falling))]
    pallas_call x0 -> x6, Pallas kernels: none -> 88.9 us  [call(): pl.pallas_call(kernel, out_shape=out_shape, in_specs=in_specs, out_specs=...]
    reshape x9 -> x4, local copies, waits for them, and re-layouts: 63.9 us -> 0.09 us  [the longest x1 0.08 us: local(): jnp.stack([buffer, slot], axis=1).reshape(-1)]
    ppermute x6 -> x16, starting transfers between devices: 15.5 us -> 46 us  [the longest x3 17.6 us: local(): lax.ppermute(shares[d], 'clip', swaps[d])]
    reduce_sum x8 -> x0, other arithmetic: 23.1 us -> none  [the longest x1 19.2 us: attend(): jnp.sum(far_exp, axis=-1, keepdims=True)]
    convert_element_type x3 -> x0, local copies, waits for them, and re-layouts: 13.5 us -> none  [the longest x1 6.13 us: attend(): result.reshape(frame_count, cell_count, channels).astype(jnp.bfloat16)]
  transfers between devices with their start and end apart: 7 -> 16, of which waited for: 1 -> 11; matrix products, arithmetic and copies ran while one was open for 12% -> 2% of each run, Pallas kernels for 0% -> 0%
where the time goes in v1:
time: 263 us
  waiting for transfers between devices  109 us (41%)
  Pallas kernels  88.9 us (34%)
  starting transfers between devices  46 us (17%)
  local copies, waits for them, and re-layouts  13 us (5%)
  other arithmetic  4.33 us (2%)
    pallas_call x6, Pallas kernels, call(): pl.pallas_call(kernel, out_shape=out_shape, in_specs=in_specs, out_specs=...  88.9 us
    ppermute x3, waiting for transfers between devices, local(): above.append(lax.ppermute(above[-1], 'clip', falling))  56.9 us
    ppermute x3, waiting for transfers between devices, local(): lax.ppermute(attended[d], 'clip', swaps[d])  21.9 us
    ppermute x3, waiting for transfers between devices, local(): lax.ppermute(shares[d], 'clip', swaps[d])  21.3 us
    ppermute x3, starting transfers between devices, local(): lax.ppermute(shares[d], 'clip', swaps[d])  17.6 us
    ppermute x3, starting transfers between devices, local(): below.append(lax.ppermute(below[-1], 'clip', rising))  13.8 us
    unnamed x40, local copies, waits for them, and re-layouts  7.96 us
    ppermute x2, waiting for transfers between devices, share_tile(): got = lax.ppermute(msg, 'tile', [(0, 1), (1, 0)])  6.45 us
  transfers between devices with their start and end apart: 16, of which 11 were waited for; matrix products, arithmetic and copies ran while one was open for 2% of the time, Pallas kernels for 0%

profile of v1, /device:TPU:0, one launch (start us, length us, event | category | flops | bytes accessed | tf_op | source)
XLA Modules:
  0.0 262.6 jit_solution(15776291921683236409)
XLA Ops:
  4.4 3.0 %collective-permute-start = (bf16[2,80,320]{2,1,0:T(8,128)(2,1)S(1)}, bf16[2,80,320]{2,1,0:T(8,128)(2,1)S(1)}, u32[]{:S(2)}, u32[]{:S(2)}) collective-permute-start(bf16[2,80,320]{2,1,0:T(8,128)(2,1)S(1)} %get-tuple-element.24), channel_id=1, source_target_pairs={{0,1},{1,0},{2,3},{3,2},{4,5},{5,4},{6,7},{7,6},{8,9},{9,8},{10,11... | collective-permute-start | bytes 307208 | tf_op jit(solution)/shard_map/ppermute | solution.py:357
  7.5 3.3 %collective-permute-done.top_ref.bottom_ref = bf16[2,80,320]{2,1,0:T(8,128)(2,1)S(1)} collective-permute-done((bf16[2,80,320]{2,1,0:T(8,128)(2,1)S(1)}, bf16[2,80,320]{2,1,0:T(8,128)(2,1)S(1)}, u32[]{:S(2)}, u32[]{:S(2)}) %collective-permute-start) | collective-permute-done | bytes 102432 | tf_op jit(solution)/shard_map/ppermute | solution.py:357
  10.8 14.1 %conv_one.1 = (bf16[2,1280,320]{2,1,0:T(8,128)(2,1)S(1)}, f32[2,8,320]{2,1,0:T(8,128)S(1)}, bf16[2,80,320]{2,1,0:T(8,128)(2,1)S(1)}) custom-call(s32[28]{0:T(128)S(1)} %concatenate.3.scalars, bf16[2,1280,320]{2,1,0:T(8,128)(2,1)S(1)} %bitcast.14, f32[2,8,320]{2,1,0:T(8,128)S(1)} %get-tuple-element.23.stats_ref, ...), custom_call_target="tpu_custom_call" | custom-call | flops 4718592000 | bytes 5469552 | tf_op jit(solution)/shard_map/conv_one/pallas_call | solution.py:30
  26.2 1.7 collective-permute-start.1
  27.9 3.1 %collective-permute-done.1.top_ref.bottom_ref = bf16[2,80,320]{2,1,0:T(8,128)(2,1)S(1)} collective-permute-done((bf16[2,80,320]{2,1,0:T(8,128)(2,1)S(1)}, bf16[2,80,320]{2,1,0:T(8,128)(2,1)S(1)}, u32[]{:S(2)}, u32[]{:S(2)}) %collective-permute-start.1) | collective-permute-done | bytes 102432 | tf_op jit(solution)/shard_map/ppermute | solution.py:357
  31.1 16.0 %conv_two.1 = (bf16[2,1280,320]{2,1,0:T(8,128)(2,1)S(1)}, bf16[2,1280,320]{2,1,0:T(8,128)(2,1)S(1)}, bf16[1280,320]{1,0:T(8,128)(2,1)S(1)}, bf16[1280,320]{1,0:T(8,128)(2,1)S(1)}) custom-call(s32[28]{0:T(128)S(1)} %concatenate.3.scalars, bf16[2,1280,320]{2,1,0:T(8,128)(2,1)} %copy-done.9, f32[2,8,320]{2,1,0:T(8,128)S(1)} %get-tuple-element.26.stats_ref, ...), custom_call_target="tpu_custom_call" | custom-call | flops 4718592000 | bytes 10261872 | tf_op jit(solution)/shard_map/conv_two/pallas_call | solution.py:30
  53.2 3.0 %collective-permute-start.2 = (bf16[1280,320]{0,1:T(8,128)(2,1)}, bf16[1280,320]{0,1:T(8,128)(2,1)}, u32[]{:S(2)}, u32[]{:S(2)}) collective-permute-start(bf16[1280,320]{0,1:T(8,128)(2,1)} %copy.15), channel_id=1, source_target_pairs={{0,2},{2,0},{4,6},{6,4},{8,10},{10,8},{12,14},{14,12},{16,18},{18,... | collective-permute-start | bytes 2457608 | tf_op jit(solution)/shard_map/ppermute | solution.py:450
  56.9 1.6 collective-permute-done.2
  60.1 6.9 %time_mix.1 = (bf16[2,1280,320]{2,1,0:T(8,128)(2,1)}, bf16[2,336,320]{2,1,0:T(8,128)(2,1)S(1)}, bf16[2,336,320]{2,1,0:T(8,128)(2,1)}, bf16[2,336,320]{2,1,0:T(8,128)(2,1)S(1)}, bf16[2,336,320]{2,1,0:T(8,128)(2,1)S(1)}) custom-call(s32[28]{0:T(128)S(1)} %concatenate.3.scalars, bf16[2,1280,320]{2,1,0:T(8,128)(2,1)} %copy-done.2, ...), custom_call_target="tpu_custom_call" | custom-call | flops 1572864000 | bytes 8889712 | tf_op jit(solution)/shard_map/time_mix/pallas_call | solution.py:30
  68.5 15.2 %collective-permute-start.4 = (bf16[2,336,320]{2,1,0:T(8,128)(2,1)}, bf16[2,336,320]{2,1,0:T(8,128)(2,1)S(1)}, u32[]{:S(2)}, u32[]{:S(2)}) collective-permute-start(bf16[2,336,320]{2,1,0:T(8,128)(2,1)} %get-tuple-element.34), channel_id=1, source_target_pairs={{0,2},{2,0},{4,6},{6,4},{8,10},{10,8},{12,14},{14,12},{16,18},{18,... | collective-permute-start | bytes 1290248 | tf_op jit(solution)/shard_map/ppermute | solution.py:465
  84.5 2.3 collective-permute-start.5
  88.3 11.2 %collective-permute-done.5.rest_2_ = bf16[2,336,320]{2,1,0:T(8,128)(2,1)S(1)} collective-permute-done((bf16[2,336,320]{2,1,0:T(8,128)(2,1)}, bf16[2,336,320]{2,1,0:T(8,128)(2,1)S(1)}, u32[]{:S(2)}, u32[]{:S(2)}) %collective-permute-start.5) | collective-permute-done | bytes 430112 | tf_op jit(solution)/shard_map/ppermute | solution.py:465
  100.1 10.1 %collective-permute-done.6.rest_3_ = bf16[2,336,320]{2,1,0:T(8,128)(2,1)S(1)} collective-permute-done((bf16[2,336,320]{2,1,0:T(8,128)(2,1)}, bf16[2,336,320]{2,1,0:T(8,128)(2,1)S(1)}, u32[]{:S(2)}, u32[]{:S(2)}) %collective-permute-start.6) | collective-permute-done | bytes 430112 | tf_op jit(solution)/shard_map/ppermute | solution.py:465
  112.6 4.6 %collective-permute-start.7 = (bf16[4,320,320]{2,1,0:T(8,128)(2,1)S(1)}, bf16[4,320,320]{2,1,0:T(8,128)(2,1)S(1)}, u32[]{:S(2)}, u32[]{:S(2)}) collective-permute-start(bf16[4,320,320]{2,1,0:T(8,128)(2,1)S(1)} %pad_maximum_fusion.rest_4_), channel_id=1, source_target_pairs={{0,8},{2,10},{4,12},{6,14},{8,16},{10,18},{12,20},{14,22},{16,24},... | collective-permute-start | bytes 2457608 | tf_op jit(solution)/shard_map/ppermute | solution.py:477
  117.2 19.8 %collective-permute-done.10.rest_8_ = bf16[4,320,320]{2,1,0:T(8,128)(2,1)S(1)} collective-permute-done((bf16[4,320,320]{2,1,0:T(8,128)(2,1)S(1)}, bf16[4,320,320]{2,1,0:T(8,128)(2,1)S(1)}, u32[]{:S(2)}, u32[]{:S(2)}) %collective-permute-start.10) | collective-permute-done | bytes 819232 | tf_op jit(solution)/shard_map/ppermute | solution.py:478
  138.3 4.6 %collective-permute-start.8 = (bf16[4,320,320]{2,1,0:T(8,128)(2,1)S(1)}, bf16[4,320,320]{2,1,0:T(8,128)(2,1)S(1)}, u32[]{:S(2)}, u32[]{:S(2)}) collective-permute-start(bf16[4,320,320]{2,1,0:T(8,128)(2,1)S(1)} %collective-permute-done.7.rest_5_), channel_id=1, source_target_pairs={{0,8},{2,10},{4,12},{6,14},{8,16},{10,18},{12,20},{14,22},{16,24},... | collective-permute-start | bytes 2457608 | tf_op jit(solution)/shard_map/ppermute | solution.py:477
  142.9 18.9 %collective-permute-done.11.rest_9_ = bf16[4,320,320]{2,1,0:T(8,128)(2,1)S(1)} collective-permute-done((bf16[4,320,320]{2,1,0:T(8,128)(2,1)S(1)}, bf16[4,320,320]{2,1,0:T(8,128)(2,1)S(1)}, u32[]{:S(2)}, u32[]{:S(2)}) %collective-permute-start.11) | collective-permute-done | bytes 819232 | tf_op jit(solution)/shard_map/ppermute | solution.py:478
  163.1 4.6 %collective-permute-start.9 = (bf16[4,320,320]{2,1,0:T(8,128)(2,1)S(1)}, bf16[4,320,320]{2,1,0:T(8,128)(2,1)S(1)}, u32[]{:S(2)}, u32[]{:S(2)}) collective-permute-start(bf16[4,320,320]{2,1,0:T(8,128)(2,1)S(1)} %collective-permute-done.8.rest_6_), channel_id=1, source_target_pairs={{0,8},{2,10},{4,12},{6,14},{8,16},{10,18},{12,20},{14,22},{16,24},... | collective-permute-start | bytes 2457608 | tf_op jit(solution)/shard_map/ppermute | solution.py:477
  167.7 18.3 %collective-permute-done.12.rest_10_ = bf16[4,320,320]{2,1,0:T(8,128)(2,1)S(1)} collective-permute-done((bf16[4,320,320]{2,1,0:T(8,128)(2,1)S(1)}, bf16[4,320,320]{2,1,0:T(8,128)(2,1)S(1)}, u32[]{:S(2)}, u32[]{:S(2)}) %collective-permute-start.12) | collective-permute-done | bytes 819232 | tf_op jit(solution)/shard_map/ppermute | solution.py:478
  188.2 47.4 %attend.1 = (bf16[2,320,320]{2,1,0:T(8,128)(2,1)S(1)}, bf16[2,320,320]{2,1,0:T(8,128)(2,1)S(1)}, bf16[2,320,320]{2,1,0:T(8,128)(2,1)S(1)}, bf16[2,320,320]{2,1,0:T(8,128)(2,1)S(1)}) custom-call(s32[28]{0:T(128)S(1)} %concatenate.3.scalars, bf16[2,336,320]{2,1,0:T(8,128)(2,1)S(1)} %get-tuple-element.33.rest_0_, ...), custom_call_target="tpu_custom_call" | custom-call | flops 5242880000 | bytes 9707632 | tf_op jit(solution)/shard_map/attend/pallas_call | solution.py:30
  235.7 1.7 collective-permute-start.14
  237.5 12.2 %collective-permute-done.14.rest_2_ = bf16[2,320,320]{2,1,0:T(8,128)(2,1)S(1)} collective-permute-done((bf16[2,320,320]{2,1,0:T(8,128)(2,1)S(1)}, bf16[2,320,320]{2,1,0:T(8,128)(2,1)S(1)}, u32[]{:S(2)}, u32[]{:S(2)}) %collective-permute-start.14) | collective-permute-done | bytes 409632 | tf_op jit(solution)/shard_map/ppermute | solution.py:497
  249.8 9.6 %collective-permute-done.15.rest_3_ = bf16[2,320,320]{2,1,0:T(8,128)(2,1)S(1)} collective-permute-done((bf16[2,320,320]{2,1,0:T(8,128)(2,1)S(1)}, bf16[2,320,320]{2,1,0:T(8,128)(2,1)S(1)}, u32[]{:S(2)}, u32[]{:S(2)}) %collective-permute-start.15) | collective-permute-done | bytes 409632 | tf_op jit(solution)/shard_map/ppermute | solution.py:497
  259.4 3.2 %project.1 = bf16[2,1280,320]{2,1,0:T(8,128)(2,1)} custom-call(s32[28]{0:T(128)S(1)} %concatenate.3.scalars, bf16[2,1280,320]{2,1,0:T(8,128)(2,1)S(1)} %copy-done.1, bf16[2,320,320]{2,1,0:T(8,128)(2,1)S(1)} %get-tuple-element.37.rest_0_, bf16[2,320,320]{2,1,0:T(8,128)(2,1)S(1)} %collective-permute-done.13.rest_1_, ...), custom_call_target="tpu_custom_call" | custom-call | flops 524288000 | bytes 5120112 | tf_op jit(solution)/shard_map/project/pallas_call | solution.py:30
  (75 shorter events, 25.1 us)
Async XLA Ops:
  4.4 6.4 %collective-permute-start = (bf16[2,80,320]{2,1,0:T(8,128)(2,1)S(1)}, bf16[2,80,320]{2,1,0:T(8,128)(2,1)S(1)}, u32[]{:S(2)}, u32[]{:S(2)}) collective-permute-start(bf16[2,80,320]{2,1,0:T(8,128)(2,1)S(1)} %get-tuple-element.24), channel_id=1, source_target_pairs={{0,1},{1,0},{2,3},{3,2},{4,5},{5,4},{6,7},{7,6},{8,9},{9,8},{10,11... | collective-permute-start | bytes 307208 | tf_op jit(solution)/shard_map/ppermute | solution.py:357
  26.2 4.9 %collective-permute-start.1 = (bf16[2,80,320]{2,1,0:T(8,128)(2,1)S(1)}, bf16[2,80,320]{2,1,0:T(8,128)(2,1)S(1)}, u32[]{:S(2)}, u32[]{:S(2)}) collective-permute-start(bf16[2,80,320]{2,1,0:T(8,128)(2,1)S(1)} %get-tuple-element.27), channel_id=1, source_target_pairs={{0,1},{1,0},{2,3},{3,2},{4,5},{5,4},{6,7},{7,6},{8,9},{9,8},{10,11... | collective-permute-start | bytes 307208 | tf_op jit(solution)/shard_map/ppermute | solution.py:357
  51.0 5.3 %collective-permute-start.3 = (bf16[1280,320]{0,1:T(8,128)(2,1)}, bf16[1280,320]{0,1:T(8,128)(2,1)S(1)}, u32[]{:S(2)}, u32[]{:S(2)}) collective-permute-start(bf16[1280,320]{0,1:T(8,128)(2,1)} %copy.16), channel_id=1, source_target_pairs={{2,4},{6,8},{10,12},{14,16},{18,20},{22,24},{26,28},{4,2},{8,6},{1... | collective-permute-start | bytes 2457608 | tf_op jit(solution)/shard_map/ppermute | solution.py:451
  53.2 5.3 %collective-permute-start.2 = (bf16[1280,320]{0,1:T(8,128)(2,1)}, bf16[1280,320]{0,1:T(8,128)(2,1)}, u32[]{:S(2)}, u32[]{:S(2)}) collective-permute-start(bf16[1280,320]{0,1:T(8,128)(2,1)} %copy.15), channel_id=1, source_target_pairs={{0,2},{2,0},{4,6},{6,4},{8,10},{10,8},{12,14},{14,12},{16,18},{18,... | collective-permute-start | bytes 2457608 | tf_op jit(solution)/shard_map/ppermute | solution.py:450
  60.1 23.7 %copy-start.13 = (s32[8]{0:T(128)S(1)}, s32[8]{0:T(128)}, u32[]{:S(2)}) copy-start(s32[8]{0:T(128)} %param.13) | copy-start | bytes 100
  68.5 19.0 %collective-permute-start.4 = (bf16[2,336,320]{2,1,0:T(8,128)(2,1)}, bf16[2,336,320]{2,1,0:T(8,128)(2,1)S(1)}, u32[]{:S(2)}, u32[]{:S(2)}) collective-permute-start(bf16[2,336,320]{2,1,0:T(8,128)(2,1)} %get-tuple-element.34), channel_id=1, source_target_pairs={{0,2},{2,0},{4,6},{6,4},{8,10},{10,8},{12,14},{14,12},{16,18},{18,... | collective-permute-start | bytes 1290248 | tf_op jit(solution)/shard_map/ppermute | solution.py:465
  84.5 15.1 %collective-permute-start.5 = (bf16[2,336,320]{2,1,0:T(8,128)(2,1)}, bf16[2,336,320]{2,1,0:T(8,128)(2,1)S(1)}, u32[]{:S(2)}, u32[]{:S(2)}) collective-permute-start(bf16[2,336,320]{2,1,0:T(8,128)(2,1)} %copy-done.8), channel_id=1, source_target_pairs={{0,4},{2,6},{4,0},{6,2},{8,12},{10,14},{12,8},{14,10},{16,20},{18,... | collective-permute-start | bytes 1290248 | tf_op jit(solution)/shard_map/ppermute | solution.py:465
  86.7 23.5 %collective-permute-start.6 = (bf16[2,336,320]{2,1,0:T(8,128)(2,1)}, bf16[2,336,320]{2,1,0:T(8,128)(2,1)S(1)}, u32[]{:S(2)}, u32[]{:S(2)}) collective-permute-start(bf16[2,336,320]{2,1,0:T(8,128)(2,1)} %copy-done.7), channel_id=1, source_target_pairs={{0,6},{2,4},{4,2},{6,0},{8,14},{10,12},{12,10},{14,8},{16,22},{18,... | collective-permute-start | bytes 1290248 | tf_op jit(solution)/shard_map/ppermute | solution.py:465
  87.6 100.5 %copy-start.6 = (bf16[320,960]{1,0:T(8,128)(2,1)S(1)}, bf16[320,960]{1,0:T(8,128)(2,1)}, u32[]{:S(2)}) copy-start(bf16[320,960]{1,0:T(8,128)(2,1)} %rest_11_.1) | copy-start | bytes 1843204
  111.1 148.3 %copy-start.1 = (bf16[2,1280,320]{2,1,0:T(8,128)(2,1)S(1)}, bf16[2,1280,320]{2,1,0:T(8,128)(2,1)}, u32[]{:S(2)}) copy-start(bf16[2,1280,320]{2,1,0:T(8,128)(2,1)} %get-tuple-element.32.res_ref) | copy-start | bytes 4915204
  111.1 148.3 %copy-start.5 = (bf16[320,320]{1,0:T(8,128)(2,1)S(1)}, bf16[320,320]{1,0:T(8,128)(2,1)}, u32[]{:S(2)}) copy-start(bf16[320,320]{1,0:T(8,128)(2,1)} %rest_4_.1) | copy-start | bytes 614404
  111.1 25.8 %collective-permute-start.10 = (bf16[4,320,320]{2,1,0:T(8,128)(2,1)S(1)}, bf16[4,320,320]{2,1,0:T(8,128)(2,1)S(1)}, u32[]{:S(2)}, u32[]{:S(2)}) collective-permute-start(bf16[4,320,320]{2,1,0:T(8,128)(2,1)S(1)} %pad_maximum_fusion.rest_4_), channel_id=1, source_target_pairs={{8,0},{10,2},{12,4},{14,6},{16,8},{18,10},{20,12},{22,14},{24,16},... | collective-permute-start | bytes 2457608 | tf_op jit(solution)/shard_map/ppermute | solution.py:478
  112.6 25.7 %collective-permute-start.7 = (bf16[4,320,320]{2,1,0:T(8,128)(2,1)S(1)}, bf16[4,320,320]{2,1,0:T(8,128)(2,1)S(1)}, u32[]{:S(2)}, u32[]{:S(2)}) collective-permute-start(bf16[4,320,320]{2,1,0:T(8,128)(2,1)S(1)} %pad_maximum_fusion.rest_4_), channel_id=1, source_target_pairs={{0,8},{2,10},{4,12},{6,14},{8,16},{10,18},{12,20},{14,22},{16,24},... | collective-permute-start | bytes 2457608 | tf_op jit(solution)/shard_map/ppermute | solution.py:477
  136.9 50.2 %copy-start.14 = (bf16[4,320,320]{2,1,0:T(8,128)(2,1)}, bf16[4,320,320]{2,1,0:T(8,128)(2,1)S(1)}, u32[]{:S(2)}) copy-start(bf16[4,320,320]{2,1,0:T(8,128)(2,1)S(1)} %collective-permute-done.10.rest_8_) | copy-start | bytes 2457604
  136.9 24.8 %collective-permute-start.11 = (bf16[4,320,320]{2,1,0:T(8,128)(2,1)S(1)}, bf16[4,320,320]{2,1,0:T(8,128)(2,1)S(1)}, u32[]{:S(2)}, u32[]{:S(2)}) collective-permute-start(bf16[4,320,320]{2,1,0:T(8,128)(2,1)S(1)} %collective-permute-done.10.rest_8_), channel_id=1, source_target_pairs={{8,0},{10,2},{12,4},{14,6},{16,8},{18,10},{20,12},{22,14},{24,16},... | collective-permute-start | bytes 2457608 | tf_op jit(solution)/shard_map/ppermute | solution.py:478
  138.2 48.9 %copy-start.15 = (bf16[4,320,320]{2,1,0:T(8,128)(2,1)}, bf16[4,320,320]{2,1,0:T(8,128)(2,1)S(1)}, u32[]{:S(2)}) copy-start(bf16[4,320,320]{2,1,0:T(8,128)(2,1)S(1)} %collective-permute-done.7.rest_5_) | copy-start | bytes 2457604
  138.3 24.8 %collective-permute-start.8 = (bf16[4,320,320]{2,1,0:T(8,128)(2,1)S(1)}, bf16[4,320,320]{2,1,0:T(8,128)(2,1)S(1)}, u32[]{:S(2)}, u32[]{:S(2)}) collective-permute-start(bf16[4,320,320]{2,1,0:T(8,128)(2,1)S(1)} %collective-permute-done.7.rest_5_), channel_id=1, source_target_pairs={{0,8},{2,10},{4,12},{6,14},{8,16},{10,18},{12,20},{14,22},{16,24},... | collective-permute-start | bytes 2457608 | tf_op jit(solution)/shard_map/ppermute | solution.py:477
  161.8 25.4 %copy-start.16 = (bf16[4,320,320]{2,1,0:T(8,128)(2,1)}, bf16[4,320,320]{2,1,0:T(8,128)(2,1)S(1)}, u32[]{:S(2)}) copy-start(bf16[4,320,320]{2,1,0:T(8,128)(2,1)S(1)} %collective-permute-done.11.rest_9_) | copy-start | bytes 2457604
  161.8 24.2 %collective-permute-start.12 = (bf16[4,320,320]{2,1,0:T(8,128)(2,1)S(1)}, bf16[4,320,320]{2,1,0:T(8,128)(2,1)S(1)}, u32[]{:S(2)}, u32[]{:S(2)}) collective-permute-start(bf16[4,320,320]{2,1,0:T(8,128)(2,1)S(1)} %collective-permute-done.11.rest_9_), channel_id=1, source_target_pairs={{8,0},{10,2},{12,4},{14,6},{16,8},{18,10},{20,12},{22,14},{24,16},... | collective-permute-start | bytes 2457608 | tf_op jit(solution)/shard_map/ppermute | solution.py:478
  163.1 24.1 %copy-start.17 = (bf16[4,320,320]{2,1,0:T(8,128)(2,1)}, bf16[4,320,320]{2,1,0:T(8,128)(2,1)S(1)}, u32[]{:S(2)}) copy-start(bf16[4,320,320]{2,1,0:T(8,128)(2,1)S(1)} %collective-permute-done.8.rest_6_) | copy-start | bytes 2457604
  163.1 24.1 %collective-permute-start.9 = (bf16[4,320,320]{2,1,0:T(8,128)(2,1)S(1)}, bf16[4,320,320]{2,1,0:T(8,128)(2,1)S(1)}, u32[]{:S(2)}, u32[]{:S(2)}) collective-permute-start(bf16[4,320,320]{2,1,0:T(8,128)(2,1)S(1)} %collective-permute-done.8.rest_6_), channel_id=1, source_target_pairs={{0,8},{2,10},{4,12},{6,14},{8,16},{10,18},{12,20},{14,22},{16,24},... | collective-permute-start | bytes 2457608 | tf_op jit(solution)/shard_map/ppermute | solution.py:477
  235.6 1.9 collective-permute-start.13
  235.7 14.1 %collective-permute-start.14 = (bf16[2,320,320]{2,1,0:T(8,128)(2,1)S(1)}, bf16[2,320,320]{2,1,0:T(8,128)(2,1)S(1)}, u32[]{:S(2)}, u32[]{:S(2)}) collective-permute-start(bf16[2,320,320]{2,1,0:T(8,128)(2,1)S(1)} %get-tuple-element.39), channel_id=1, source_target_pairs={{0,4},{2,6},{4,0},{6,2},{8,12},{10,14},{12,8},{14,10},{16,20},{18,... | collective-permute-start | bytes 1228808 | tf_op jit(solution)/shard_map/ppermute | solution.py:497
  237.3 22.1 %collective-permute-start.15 = (bf16[2,320,320]{2,1,0:T(8,128)(2,1)S(1)}, bf16[2,320,320]{2,1,0:T(8,128)(2,1)S(1)}, u32[]{:S(2)}, u32[]{:S(2)}) collective-permute-start(bf16[2,320,320]{2,1,0:T(8,128)(2,1)S(1)} %get-tuple-element.40), channel_id=1, source_target_pairs={{0,6},{2,4},{4,2},{6,0},{8,14},{10,12},{12,10},{14,8},{16,22},{18,... | collective-permute-start | bytes 1228808 | tf_op jit(solution)/shard_map/ppermute | solution.py:497
  (12 other events, 47.2 us)
